TPU v7x, 256 devices: a whole 4x4x8 slice. The times are simulated.
256 devices in a mesh: hid: 64 (over y, z_lo, x), mdl: 4 (over z_hi, core).
Axes of the slice: x: 4, y: 4, z: 8 (z_hi: 2, z_lo: 4; z = z_hi * 4 + z_lo), core: 2. Of those that a mesh axis runs over, the one named last changes fastest.
Arguments:
- quant_input: bfloat16 [512, 8192], P('hid', 'mdl'), may hold values from -4 to 4
- input_scale: float32 [512], P('hid'), may hold values from 0.25 to 4
- grad_output: bfloat16 [512, 8192], P('hid', 'mdl'), may hold values from -0.625 to 0.625
- gate_quant: bfloat16 [8192, 28672], P('mdl', 'hid'), may hold values from -0.0625 to 0.0625
- gate_scale: float32 [28672], P('hid'), may hold values from 0.5 to 2
- up_quant: bfloat16 [8192, 28672], P('mdl', 'hid'), may hold values from -0.0625 to 0.0625
- up_scale: float32 [28672], P('hid'), may hold values from 0.5 to 2
- down_quant: bfloat16 [28672, 8192], P('hid', 'mdl'), may hold values from -0.0625 to 0.0625
- down_scale: float32 [28672], P('hid'), may hold values from 0.5 to 2
Outputs:
- input_grad: bfloat16 [512, 8192], P('hid', 'mdl')
- gate_grad: bfloat16 [8192, 28672], P('mdl', 'hid')
- up_grad: bfloat16 [8192, 28672], P('mdl', 'hid')
- down_grad: bfloat16 [28672, 8192], P('hid', 'mdl')
All inputs are finite; a program needn't handle non-finite values.
Results may differ from a plain program's by a relative error of at most 0.0092.
Values may be sent and summed in bfloat16 or wider, within the bound.
A program may use at most 64 MiB of HBM per device.

v0:
```python
import jax
import jax.numpy as jnp
from jax import lax
from jax.sharding import PartitionSpec as P


def activate(gate_sum, up_sum, hidden_grad):
    gate_sigmoid = jax.nn.sigmoid(gate_sum)
    hidden = (gate_sum * gate_sigmoid * up_sum).astype(jnp.bfloat16)
    gate_delta = (
        hidden_grad * up_sum * gate_sigmoid * (1.0 + gate_sum * (1.0 - gate_sigmoid))
    ).astype(jnp.bfloat16)
    up_delta = (hidden_grad * gate_sum * gate_sigmoid).astype(jnp.bfloat16)
    return (hidden, gate_delta, up_delta)


def contract_rows(left, right):
    return lax.dot_general(
        left, right, (((0,), (0,)), ((), ())), preferred_element_type=jnp.float32
    )


def contract_cols(left, right):
    return lax.dot_general(
        left, right, (((1,), (1,)), ((), ())), preferred_element_type=jnp.float32
    )


def local(
    quant_input,
    input_scale,
    grad_output,
    gate_quant,
    gate_scale,
    up_quant,
    up_scale,
    down_quant,
    down_scale,
):
    activations = (quant_input.astype(jnp.float32) * input_scale[:, None]).astype(jnp.bfloat16)
    gate_weight = (gate_quant.astype(jnp.float32) * gate_scale).astype(jnp.bfloat16)
    up_weight = (up_quant.astype(jnp.float32) * up_scale).astype(jnp.bfloat16)
    down_weight = (down_quant.astype(jnp.float32) * down_scale[:, None]).astype(jnp.bfloat16)
    gathered_act, gathered_grad = (
        lax.all_gather(activations, "hid", axis=0, tiled=True),
        lax.all_gather(grad_output, "hid", axis=0, tiled=True),
    )
    gate_part = jnp.dot(gathered_act, gate_weight, preferred_element_type=jnp.float32)
    up_part = jnp.dot(gathered_act, up_weight, preferred_element_type=jnp.float32)
    hidden_part = contract_cols(gathered_grad, down_weight)
    gate_sum, up_sum, hidden_grad = lax.psum((gate_part, up_part, hidden_part), "mdl")
    hidden, gate_delta, up_delta = activate(gate_sum, up_sum, hidden_grad)
    gate_grad = contract_rows(gathered_act, gate_delta).astype(jnp.bfloat16)
    up_grad = contract_rows(gathered_act, up_delta).astype(jnp.bfloat16)
    down_grad = contract_rows(hidden, gathered_grad).astype(jnp.bfloat16)
    partial_input = contract_cols(gate_delta, gate_weight) + contract_cols(up_delta, up_weight)
    input_total = lax.psum_scatter(partial_input, "hid", scatter_dimension=0, tiled=True)
    return (input_total.astype(jnp.bfloat16), gate_grad, up_grad, down_grad)


def solution(mesh):
    in_specs = (
        P("hid", "mdl"),
        P("hid"),
        P("hid", "mdl"),
        P("mdl", "hid"),
        P("hid"),
        P("mdl", "hid"),
        P("hid"),
        P("hid", "mdl"),
        P("hid"),
    )
    out_specs = (P("hid", "mdl"), P("mdl", "hid"), P("mdl", "hid"), P("hid", "mdl"))
    return jax.shard_map(local, mesh=mesh, in_specs=in_specs, out_specs=out_specs, check_vma=False)
```

profile of v0, /device:TPU:6, one launch (start us, length us, event | category | flops | bytes accessed | tf_op | source)
XLA Modules:
  0.0 1213.9 jit_solution(12678688516183394927)
XLA Ops:
  7.2 0.0 all-gather.5.cloned.1.call-start
  7.2 1.4 multiply_convert_fusion.14
  8.7 0.0 all-gather.5.cloned.1.call-update
  8.7 0.0 all-gather.3.cloned.1.call-start
  8.7 0.7 all-gather.3.cloned.1.call-update
  9.4 0.0 copy-start.1
  9.4 0.0 copy-start.6
  9.5 0.0 all-reduce.3.cloned.1.call-start
  9.5 345.9 %all-gather.5.cloned.1.call-done = bf16[512,2048]{1,0:T(8,128)(2,1)} async-done(((bf16[8,2048]{1,0:T(8,128)(2,1)}), bf16[512,2048]{1,0:T(8,128)(2,1)}) %all-gather.5.cloned.1.call-update) | async-done | bytes 2097168 | tf_op jit(solution)/shard_map/all_gather | solution.py:45
  355.4 0.0 copy-start.7
  355.4 4.4 fusion.5
  359.8 0.0 copy-done.1
  359.8 0.0 copy-done.6
  359.8 0.0 copy-done.7
  359.8 0.0 copy-start.10
  359.8 2.1 fusion.3
  361.9 342.6 %all-gather.3.cloned.1.call-done = bf16[512,2048]{1,0:T(8,128)(2,1)} async-done(((bf16[8,2048]{1,0:T(8,128)(2,1)}), bf16[512,2048]{1,0:T(8,128)(2,1)}) %all-gather.3.cloned.1.call-update) | async-done | bytes 2097168 | tf_op jit(solution)/shard_map/all_gather | solution.py:46
  704.6 0.0 copy-done.10
  704.6 4.2 fusion.2
  708.8 0.0 all-reduce.3.cloned.1.call-update
  708.8 0.0 copy-start
  708.9 0.0 copy-start.5
  708.9 0.0 reduce-scatter.2.cloned.1.call-start
  708.9 127.6 %all-reduce.3.cloned.1.call-done = (f32[512,448]{0,1:T(8,128)}, f32[512,448]{0,1:T(8,128)}, f32[512,448]{0,1:T(8,128)}) async-done(((f32[512,448]{0,1:T(8,128)}, f32[512,448]{0,1:T(8,128)}, f32[512,448]{0,1:T(8,128)}), (f32[512,448]{0,1:T(8,128)}, f32[512,448]{0,1:T(8,128)}, f32[512,448]{0,1:T(8,128)})) %all-reduce.3.cloned.1.call-update) | async-done | bytes 2752528 | tf_op jit(solution)/shard_map/psum | solution.py:51
  836.5 2.2 multiply_convert_fusion.7
  838.8 0.0 copy-done
  838.8 0.0 copy-done.5
  838.8 0.0 copy-start.2
  838.8 1.4 fusion.4
  840.2 0.1 copy-done.2
  840.3 3.4 convolution_add_fusion
  843.8 0.0 copy-start.8
  843.8 0.0 reduce-scatter.2.cloned.1.call-update
  843.8 1.6 copy-done.8
  845.4 2.4 convolution_convert_fusion
  847.7 0.0 copy-start.3
  847.7 0.0 copy-start.4
  847.7 0.0 copy-start.9
  847.7 2.4 convolution_convert_fusion.1
  850.1 0.0 copy-done.3
  850.1 0.0 copy-done.4
  850.1 0.0 copy-done.9
  850.1 2.4 convolution_convert_fusion.2
  852.5 353.4 %reduce-scatter.2.cloned.1.call-done = f32[8,2048]{1,0:T(8,128)} async-done(((f32[512,2048]{1,0:T(8,128)}), f32[8,2048]{1,0:T(8,128)}) %reduce-scatter.2.cloned.1.call-update) | async-done | bytes 65552 | tf_op jit(solution)/shard_map/reduce_scatter | solution.py:57
  1205.9 1.5 convert_element_type.55
Async XLA Ops:
  7.2 348.2 %all-gather.5.cloned.1.call-start = ((), (), s32[]{:S(2)}) async-start(), calls=%async_computation.2 | async-start | bytes 2129920 | tf_op jit(solution)/shard_map/all_gather | solution.py:45
  8.7 695.9 %all-gather.3.cloned.1.call-start = ((), (), s32[]{:S(2)}) async-start(), calls=%async_computation.1 | async-start | bytes 2129920 | tf_op jit(solution)/shard_map/all_gather | solution.py:46
  9.4 350.4 %copy-start.1 = (bf16[2048,448]{0,1:T(8,128)(2,1)S(1)}, bf16[2048,448]{0,1:T(8,128)(2,1)}, u32[]{:S(2)}) copy-start(bf16[2048,448]{0,1:T(8,128)(2,1)} %param.14) | copy-start | bytes 5505028
  9.4 350.3 %copy-start.6 = (f32[448]{0:T(512)S(1)}, f32[448]{0:T(512)}, u32[]{:S(2)}) copy-start(f32[448]{0:T(512)} %param.15) | copy-start | bytes 5380
  9.5 827.1 %all-reduce.3.cloned.1.call-start = ((), (), s32[]{:S(2)}) async-start(), calls=%async_computation.4 | async-start | bytes 5505024 | tf_op jit(solution)/shard_map/psum | solution.py:51
  355.4 4.4 copy-start.7
  359.8 344.8 %copy-start.10 = (f32[448]{0:T(512)S(1)}, f32[448]{0:T(512)}, u32[]{:S(2)}) copy-start(f32[448]{0:T(512)} %param.17) | copy-start | bytes 5380
  708.8 129.9 %copy-start = (bf16[2048,448]{0,1:T(8,128)(2,1)S(1)}, bf16[2048,448]{0,1:T(8,128)(2,1)}, u32[]{:S(2)}) copy-start(bf16[2048,448]{0,1:T(8,128)(2,1)} %param.12) | copy-start | bytes 5505028
  708.9 129.9 %copy-start.5 = (f32[448]{0:T(512)S(1)}, f32[448]{0:T(512)}, u32[]{:S(2)}) copy-start(f32[448]{0:T(512)} %param.13) | copy-start | bytes 5380
  708.9 497.0 %reduce-scatter.2.cloned.1.call-start = ((), (), s32[]{:S(2)}) async-start(), calls=%async_computation.3 | async-start | bytes 4259840 | tf_op jit(solution)/shard_map/reduce_scatter | solution.py:57
  838.8 1.5 copy-start.2
  843.8 1.6 copy-start.8
  847.7 2.4 copy-start.3
  847.7 2.4 copy-start.4
  847.7 2.4 copy-start.9
Sparse Core Ops, SparseCore 0:
  10.4 345.0 all-gather.4
  357.2 347.3 all-gather.2
  709.0 127.5 all-reduce.2
  843.9 361.9 reduce-scatter.1
where the time goes:
time: 1230 us; the launch traced here: 1210 us
  waiting for transfers between devices  1170 us (95%)
  matrix products  22.6 us (2%)
  between operations  13.8 us (1%)
    reduce_scatter x1, waiting for transfers between devices, local(): lax.psum_scatter(partial_input, 'hid', scatter_dimension=0, tiled=True)  353 us
    all_gather x1, waiting for transfers between devices, local(): lax.all_gather(activations, 'hid', axis=0, tiled=True)  346 us
    all_gather x1, waiting for transfers between devices, local(): lax.all_gather(grad_output, 'hid', axis=0, tiled=True)  343 us
    psum x1, waiting for transfers between devices, local(): lax.psum((gate_part, up_part, hidden_part), 'mdl')  128 us
  transfers between devices with their start and end apart: 4, of which 4 were waited for; matrix products, arithmetic and copies ran while one was open for 1% of the time, Pallas kernels for 0%

commit v1 on v0

v1 whole, which is shorter than its diff:
```python
import jax
import jax.numpy as jnp
from jax import lax
from jax.experimental import pallas as pl
from jax.experimental.pallas import tpu as pltpu
from jax.sharding import PartitionSpec as P

MESH = pl.DeviceIdType.MESH
BF = jnp.bfloat16
F32 = jnp.float32
D = 2048
H = 448
HP = 512
TOKENS = 512


def contract_rows(left, right):
    return lax.dot_general(left, right, (((0,), (0,)), ((), ())), preferred_element_type=F32)


def contract_cols(left, right):
    return lax.dot_general(left, right, (((1,), (1,)), ((), ())), preferred_element_type=F32)


def rows_at(start, size, step):
    return pl.ds(pl.multiple_of(start, step), size)


def kernel(
    slab, gate_q, up_q, down_q, gate_s, up_s, down_s,
    dx, act, grad, delta, hidden,
    gathered, raw_g, raw_u, raw_d, w_gu, w_d, part, sib, total, z_out, z_in,
    pi_own, pi_out, r1_in, r2_own, r2_out, r2_in, r3_own, r3_out, r3_in,
    load_sem, gz, gp, gn, gf, sc, sz, sd, s1, s2, s3,
):
    hid = lax.axis_index("hid")
    mdl = lax.axis_index("mdl")
    x, z, y = hid % 4, (hid // 4) % 4, hid // 16
    core, half = mdl % 2, mdl // 2

    def at(px, py, pz):
        return ((py * 4 + pz) * 4 + px, mdl)

    def x_peer(d):
        return at((x + d) % 4, y, z)

    def y_peer(d):
        return at(x, (y + d) % 4, z)

    def z_peer(d):
        return at(x, y, (z + d) % 4)

    sibling = (hid, half * 2 + (1 - core))
    far = (hid, (1 - half) * 2 + core)

    pos = jnp.where(z < 2, (y * 4 + x) * 2 + z, 32 + (x * 4 + y) * 2 + z - 2)
    loads = [
        pltpu.make_async_copy(src, dst, load_sem.at[i])
        for i, (src, dst) in enumerate(
            [(gate_q, raw_g), (up_q, raw_u), (down_q, raw_d), (slab, gathered.at[pos])]
        )
    ]
    for c in (loads[3], loads[0], loads[1], loads[2]):
        c.start()

    barrier = pltpu.get_barrier_semaphore()
    partners = [f(d) for f in (x_peer, y_peer, z_peer) for d in (1, 2, 3)] + [sibling, far]
    for p in partners:
        pl.semaphore_signal(barrier, inc=1, device_id=p, device_id_type=MESH)
    pl.semaphore_wait(barrier, len(partners))

    sent = []

    def send(src, dst, sems, to):
        c = pltpu.make_async_remote_copy(
            src_ref=src, dst_ref=dst, send_sem=sems.at[0], recv_sem=sems.at[1],
            device_id=to, device_id_type=MESH,
        )
        c.start()
        sent.append(c)
        return c

    loads[3].wait()
    over_z = [send(gathered.at[pos], gathered.at[pos], gz.at[d - 1], z_peer(d)) for d in (1, 2, 3)]

    loads[0].wait()

    @pl.loop(0, 16)
    def _(i):
        r = rows_at(i * 128, 128, 128)
        w_gu[r, 0:H] = (raw_g[r, :].astype(F32) * gate_s[...]).astype(BF)
        w_gu[r, H:HP] = jnp.zeros((128, HP - H), BF)

    for c in over_z:
        c.wait_recv()

    unit_a = gathered.at[pl.ds((y * 4 + x) * 2, 2)]
    unit_b = gathered.at[pl.ds(32 + (x * 4 + y) * 2, 2)]
    second = []
    for d in (1, 3, 2):
        second.append(send(unit_a, unit_a, gp.at[0, d - 1], x_peer(d)))
        second.append(send(unit_b, unit_b, gp.at[1, d - 1], y_peer(d)))

    loads[1].wait()

    @pl.loop(0, 16)
    def _(i):
        r = rows_at(i * 128, 128, 128)
        w_gu[r, HP:HP + H] = (raw_u[r, :].astype(F32) * up_s[...]).astype(BF)
        w_gu[r, HP + H:] = jnp.zeros((128, HP - H), BF)

    for c in second:
        c.wait_recv()

    line_a = gathered.at[pl.ds(y * 8, 8)]
    line_b = gathered.at[pl.ds(32 + x * 8, 8)]
    third = []
    for i, d in enumerate((1, 3)):
        third.append(
            (
                send(line_a, line_a, gn.at[0, i], y_peer(d)),
                send(line_b, line_b, gn.at[1, i], x_peer(d)),
            )
        )

    loads[2].wait()

    @pl.loop(0, 7)
    def _(i):
        r = rows_at(i * 64, 64, 64)
        w_d[r, :] = (raw_d[r, :].astype(F32) * down_s[r, :]).astype(BF)

    w_d[H:HP, :] = jnp.zeros((HP - H, D), BF)

    def repack(k):
        ahead = (0, 3, 1, 2)[k]
        for line, row in (((y + ahead) % 4 * 8, 0), (32 + (x + ahead) % 4 * 8, 64)):

            @pl.loop(0, 4)
            def _(j):
                a = gathered[line + 2 * j].astype(F32)
                b = gathered[line + 2 * j + 1].astype(F32)
                r = rows_at(k * 128 + row + j * 16, 16, 16)
                act[r, :] = jnp.concatenate([a[:8], b[:8]], axis=0).astype(BF)
                grad[r, :] = jnp.concatenate([a[8:], b[8:]], axis=0).astype(BF)

    def partials(k):
        r = pl.ds(k * 128, 128)

        @pl.loop(0, 4)
        def _(j):
            c = rows_at(j * 256, 256, 256)
            part[k, :, c] = jnp.dot(act[r, :], w_gu[:, c], preferred_element_type=F32)

        @pl.loop(0, 2)
        def _(j):
            c = rows_at(j * 256, 256, 256)
            part[k, :, rows_at(2 * HP + j * 256, 256, 256)] = contract_cols(grad[r, :], w_d[c, :])

        other = rows_at((1 - core) * 64, 64, 64)
        return send(part.at[k, other], sib.at[k], sc.at[k], sibling)

    def to_far(k, arrived):
        arrived.wait_recv()
        mine = rows_at(core * 64, 64, 64)
        s = part[k, mine, :] + sib[k]
        total[k] = s
        z_out[k] = s.astype(BF)
        return send(z_out.at[k], z_in.at[k], sz.at[k], far)

    def activate(k, arrived):
        arrived.wait_recv()
        gate_sum, up_sum, hidden_grad = (
            total[k, :, i * HP:(i + 1) * HP] + z_in[k, :, i * HP:(i + 1) * HP].astype(F32)
            for i in range(3)
        )
        gate_sigmoid = jax.nn.sigmoid(gate_sum)
        mine = rows_at(k * 128 + core * 64, 64, 64)
        hidden[mine, :] = (gate_sum * gate_sigmoid * up_sum).astype(BF)
        delta[mine, 0:HP] = (
            hidden_grad * up_sum * gate_sigmoid * (1.0 + gate_sum * (1.0 - gate_sigmoid))
        ).astype(BF)
        delta[mine, HP:] = (hidden_grad * gate_sum * gate_sigmoid).astype(BF)
        return [
            send(delta.at[mine], delta.at[mine], sd.at[0, k], sibling),
            send(hidden.at[mine], hidden.at[mine], sd.at[1, k], sibling),
        ]

    def input_part(k, arrived):
        arrived[0].wait_recv()
        r = pl.ds(k * 128, 128)

        @pl.loop(0, 8)
        def _(j):
            c = rows_at(j * 256, 256, 256)
            value = contract_cols(delta[r, :], w_gu[c, :])
            if k == 0:
                pi_own[:, c] = value
            else:
                pi_out[k - 1, :, c] = value.astype(BF)

        if k == 0:
            return []
        d = (0, 3, 1, 2)[k]
        return [
            send(pi_out.at[k - 1, 0:64], r1_in.at[0, k - 1], s1.at[0, k - 1], y_peer(d)),
            send(pi_out.at[k - 1, 64:128], r1_in.at[1, k - 1], s1.at[1, k - 1], x_peer(d)),
        ]

    repack(0)
    core_copy = [partials(0)]
    far_copy = [to_far(0, core_copy[0])]

    for c in third[0]:
        c.wait_recv()
    fwd_a = gathered.at[pl.ds((y + 3) % 4 * 8, 4)]
    fwd_b = gathered.at[pl.ds(32 + (x + 3) % 4 * 8, 4)]
    fourth = [
        send(fwd_a, fwd_a, gf.at[0, 0], y_peer(1)),
        send(fwd_b, fwd_b, gf.at[1, 0], x_peer(1)),
    ]
    for c in third[1]:
        c.wait_recv()
    back_a = gathered.at[pl.ds((y + 1) % 4 * 8 + 4, 4)]
    back_b = gathered.at[pl.ds(32 + (x + 1) % 4 * 8 + 4, 4)]
    fourth += [
        send(back_a, back_a, gf.at[0, 1], y_peer(3)),
        send(back_b, back_b, gf.at[1, 1], x_peer(3)),
    ]
    repack(1)
    core_copy.append(partials(1))
    repack(2)
    far_copy.append(to_far(1, core_copy[1]))
    core_copy.append(partials(2))
    far_copy.append(to_far(2, core_copy[2]))
    for c in fourth:
        c.wait_recv()
    repack(3)
    core_copy.append(partials(3))
    far_copy.append(to_far(3, core_copy[3]))

    over_1 = []
    deltas = []
    for k in range(4):
        deltas.append(activate(k, far_copy[k]))
        over_1 += input_part(k, deltas[k])

    for c in over_1:
        c.wait_recv()
    over_2 = []
    for i, me in ((0, x), (1, y)):
        own = pi_own[i * 64:i * 64 + 64, :]
        for k in range(3):
            own = own + r1_in[i, k].astype(F32)
        r2_own[i] = own
        r2_out[i] = own.astype(BF)
        peer = (x_peer, y_peer)[i]
        for d in (2, 1, 3):
            to = rows_at((me + d) % 4 * 16, 16, 16)
            over_2.append(send(r2_out.at[i, to], r2_in.at[i, d - 1], s2.at[i, d - 1], peer(d)))
    for c in over_2:
        c.wait_recv()
    for i, me in ((0, x), (1, y)):
        own = r2_own[i, rows_at(me * 16, 16, 16), :]
        for d in range(3):
            own = own + r2_in[i, d].astype(F32)
        for j in range(2):
            own_j = own[j * 8:j * 8 + 8]
            r3_own[2 * i + j] = own_j
            r3_out[2 * i + j] = jnp.concatenate([own_j[:, :1024], own_j[:, 1024:]], axis=0).astype(BF)
    over_3 = []
    for d in (2, 1, 3):
        over_3.append(send(r3_out.at[(z + d) % 4], r3_in.at[d - 1], s3.at[d - 1], z_peer(d)))
    for c in over_3:
        c.wait_recv()
    own = r3_own[z]
    for d in range(3):
        got = r3_in[d].astype(F32)
        own = own + jnp.concatenate([got[:8], got[8:]], axis=1)
    dx[...] = own

    for pair in deltas:
        pair[1].wait_recv()
    for c in sent:
        c.wait_send()


def local(
    quant_input, input_scale, grad_output, gate_quant, gate_scale, up_quant, up_scale, down_quant, down_scale,
):
    activations = (quant_input.astype(F32) * input_scale[:, None]).astype(BF)
    slab = jnp.concatenate([activations, grad_output], axis=0)
    vmem = pl.BlockSpec(memory_space=pltpu.VMEM)
    hbm = pl.BlockSpec(memory_space=pl.ANY)
    dma = pltpu.SemaphoreType.DMA
    dx, act, grad, delta, hidden = pl.pallas_call(
        kernel,
        name="ffn_backward",
        out_shape=(
            jax.ShapeDtypeStruct((8, D), F32),
            jax.ShapeDtypeStruct((TOKENS, D), BF),
            jax.ShapeDtypeStruct((TOKENS, D), BF),
            jax.ShapeDtypeStruct((TOKENS, 2 * HP), BF),
            jax.ShapeDtypeStruct((TOKENS, HP), BF),
        ),
        in_specs=[vmem, hbm, hbm, hbm, vmem, vmem, vmem],
        out_specs=(vmem,) * 5,
        scratch_shapes=[
            pltpu.VMEM((64, 16, D), BF),
            pltpu.VMEM((D, H), BF),
            pltpu.VMEM((D, H), BF),
            pltpu.VMEM((H, D), BF),
            pltpu.VMEM((D, 2 * HP), BF),
            pltpu.VMEM((HP, D), BF),
            pltpu.VMEM((4, 128, 3 * HP), F32),
            pltpu.VMEM((4, 64, 3 * HP), F32),
            pltpu.VMEM((4, 64, 3 * HP), F32),
            pltpu.VMEM((4, 64, 3 * HP), BF),
            pltpu.VMEM((4, 64, 3 * HP), BF),
            pltpu.VMEM((128, D), F32),
            pltpu.VMEM((3, 128, D), BF),
            pltpu.VMEM((2, 3, 64, D), BF),
            pltpu.VMEM((2, 64, D), F32),
            pltpu.VMEM((2, 64, D), BF),
            pltpu.VMEM((2, 3, 16, D), BF),
            pltpu.VMEM((4, 8, D), F32),
            pltpu.VMEM((4, 16, D // 2), BF),
            pltpu.VMEM((3, 16, D // 2), BF),
            dma((4,)),
            dma((3, 2)),
            dma((2, 3, 2)),
            dma((2, 2, 2)),
            dma((2, 2, 2)),
            dma((4, 2)),
            dma((4, 2)),
            dma((2, 4, 2)),
            dma((2, 3, 2)),
            dma((2, 3, 2)),
            dma((3, 2)),
        ],
        compiler_params=pltpu.CompilerParams(
            collective_id=0, has_side_effects=True, vmem_limit_bytes=48 * 2**20
        ),
        cost_estimate=pl.CostEstimate(flops=6 * 10**9, bytes_accessed=12 * 10**6, transcendentals=300000),
    )(
        slab, gate_quant, up_quant, down_quant,
        gate_scale.reshape(1, H), up_scale.reshape(1, H), down_scale.reshape(H, 1),
    )
    gate_grad = contract_rows(act, delta[:, :H]).astype(BF)
    up_grad = contract_rows(act, delta[:, HP:HP + H]).astype(BF)
    down_grad = contract_rows(hidden[:, :H], grad).astype(BF)
    return (dx.astype(BF), gate_grad, up_grad, down_grad)


def solution(mesh):
    in_specs = (
        P("hid", "mdl"),
        P("hid"),
        P("hid", "mdl"),
        P("mdl", "hid"),
        P("hid"),
        P("mdl", "hid"),
        P("hid"),
        P("hid", "mdl"),
        P("hid"),
    )
    out_specs = (P("hid", "mdl"), P("mdl", "hid"), P("mdl", "hid"), P("hid", "mdl"))
    return jax.shard_map(local, mesh=mesh, in_specs=in_specs, out_specs=out_specs, check_vma=False)
```

time: 1230 us -> 112 us (0.09); the launches traced: 1210 us -> 112 us
  waiting for transfers between devices: 1170 us -> 0 us
  Pallas kernels: 0 us -> 91.4 us
  matrix products: 22.6 us -> 8.74 us
  between operations: 13.8 us -> 0.66 us
    all_gather x2 -> x0, waiting for transfers between devices: 689 us -> none  [the longest x1 346 us: local(): lax.all_gather(activations, 'hid', axis=0, tiled=True)]
    reduce_scatter x1 -> x0, waiting for transfers between devices: 353 us -> none  [local(): lax.psum_scatter(partial_input, 'hid', scatter_dimension=0, tiled=True)]
    psum x1 -> x0, waiting for transfers between devices: 128 us -> none  [local(): lax.psum((gate_part, up_part, hidden_part), 'mdl')]
    pallas_call x0 -> x1, Pallas kernels: none -> 91.4 us  [local(): pl.pallas_call(kernel, name='ffn_backward', out_shape=(jax.ShapeDtypeStru...]
    dot_general x5 -> x0, matrix products: 15.5 us -> none  [the longest x3 9.05 us: contract_cols(): lax.dot_general(left, right, (((1,), (1,)), ((), ())), preferred_element_...]
  transfers between devices with their start and end apart: 4 -> 0, of which waited for: 4 -> 0; matrix products, arithmetic and copies ran while one was open for 1% -> 0% of each run, Pallas kernels for 0% -> 0%
where the time goes in v1:
time: 112 us
  Pallas kernels  91.4 us (82%)
  matrix products  8.74 us (8%)
  local copies, waits for them, and re-layouts  8.57 us (8%)
  other arithmetic  2.22 us (2%)
    pallas_call x1, Pallas kernels, local(): pl.pallas_call(kernel, name='ffn_backward', out_shape=(jax.ShapeDtypeStru...  91.4 us
    dot_general x3, matrix products, contract_rows(): lax.dot_general(left, right, (((0,), (0,)), ((), ())), preferred_element_...  8.74 us
    unnamed x8, local copies, waits for them, and re-layouts  7.76 us

profile of v1, /device:TPU:6, one launch (start us, length us, event | category | flops | bytes accessed | tf_op | source)
XLA Modules:
  0.0 111.6 jit_solution(16166248704686654128)
XLA Ops:
  0.6 0.8 multiply_convert_fusion
  1.5 0.8 pad_maximum_fusion.slab
  2.2 0.8 copy.17.down_s
  3.0 3.8 %copy.15.gate_q = bf16[2048,448]{1,0:T(8,128)(2,1)} copy(bf16[2048,448]{0,1:T(8,128)(2,1)} %param.12) | data formatting | bytes 3670016 | tf_op args[3]
  6.9 0.0 copy-start
  6.9 0.0 copy-start.1
  6.9 0.0 copy-start.2
  6.9 3.9 %copy.16.up_q = bf16[2048,448]{1,0:T(8,128)(2,1)} copy(bf16[2048,448]{0,1:T(8,128)(2,1)} %param.14) | data formatting | bytes 3670016 | tf_op args[5]
  10.8 0.0 copy-done
  10.8 0.0 copy-done.1
  10.8 0.0 copy-done.2
  10.8 91.4 %ffn_backward.1 = (f32[8,2048]{1,0:T(8,128)S(1)}, bf16[512,2048]{1,0:T(8,128)(2,1)S(1)}, bf16[512,2048]{1,0:T(8,128)(2,1)}, bf16[512,1024]{1,0:T(8,128)(2,1)S(1)}, bf16[512,512]{1,0:T(8,128)(2,1)S(1)}) custom-call(bf16[16,2048]{1,0:T(8,128)(2,1)S(1)} %pad_maximum_fusion.slab, bf16[2048,448]{1,0:T(8,128)(2,1)} %copy.15.gate_q, bf16[2048,448]{1,0:T(8,128)(2,1)} %copy.16.up_q, ...), custom_call_target="tpu_custom_call" | custom-call | flops 6000000000 | bytes 12000000 | tf_op jit(solution)/shard_map/ffn_backward/pallas_call | solution.py:296
  102.2 0.6 convert_element_type.20
  102.9 4.0 %convolution_convert_fusion = bf16[448,2048]{1,0:T(8,128)(2,1)} fusion(bf16[512,2048]{1,0:T(8,128)(2,1)} %get-tuple-element.13, bf16[512,512]{1,0:T(8,128)(2,1)S(1)} %get-tuple-element.12), kind=kOutput, calls=%fused_computation | convolution fusion | flops 940441600 | bytes 4456448 | tf_op jit(solution)/shard_map/dot_general | solution.py:18
  106.8 2.4 %convolution_convert_fusion.1 = bf16[2048,448]{0,1:T(8,128)(2,1)} fusion(bf16[512,2048]{1,0:T(8,128)(2,1)S(1)} %get-tuple-element.10, bf16[512,1024]{1,0:T(8,128)(2,1)S(1)} %get-tuple-element.11), kind=kOutput, calls=%fused_computation.1 | convolution fusion | flops 940441600 | bytes 4456448 | tf_op jit(solution)/shard_map/dot_general | solution.py:18
  109.2 2.4 %convolution_convert_fusion.2 = bf16[2048,448]{0,1:T(8,128)(2,1)} fusion(bf16[512,2048]{1,0:T(8,128)(2,1)S(1)} %get-tuple-element.10, bf16[512,1024]{1,0:T(8,128)(2,1)S(1)} %get-tuple-element.11), kind=kOutput, calls=%fused_computation.2 | convolution fusion | flops 940441600 | bytes 4456448 | tf_op jit(solution)/shard_map/dot_general | solution.py:18
Async XLA Ops:
  6.9 3.9 %copy-start = (bf16[448,2048]{1,0:T(8,128)(2,1)S(1)}, bf16[448,2048]{1,0:T(8,128)(2,1)}, u32[]{:S(2)}) copy-start(bf16[448,2048]{1,0:T(8,128)(2,1)} %down_q.1) | copy-start | bytes 5505028
  6.9 3.9 %copy-start.1 = (f32[448]{0:T(512)S(1)}, f32[448]{0:T(512)}, u32[]{:S(2)}) copy-start(f32[448]{0:T(512)} %param.13) | copy-start | bytes 5380
  6.9 4.0 %copy-start.2 = (f32[448]{0:T(512)S(1)}, f32[448]{0:T(512)}, u32[]{:S(2)}) copy-start(f32[448]{0:T(512)} %param.15) | copy-start | bytes 5380

commit v2 on v0

v2 whole, which is shorter than its diff:
```python
import jax
import jax.numpy as jnp
from jax import lax
from jax.experimental import pallas as pl
from jax.experimental.pallas import tpu as pltpu
from jax.sharding import PartitionSpec as P

MESH = pl.DeviceIdType.MESH
BF = jnp.bfloat16
F32 = jnp.float32
D = 2048
H = 448
HP = 512
TOKENS = 512
PIECES = ((0, 64), (64, 64), (128, 128), (256, 128), (384, 128))
GROUPS = {
    2: ((3, 0, 4), (1, 4, 4)),
    3: ((2, 0, 8),),
    4: ((3, 4, 4), (1, 0, 4)),
}


def contract_cols(left, right):
    return lax.dot_general(left, right, (((1,), (1,)), ((), ())), preferred_element_type=F32)


def rows_at(start, size, step):
    return pl.ds(pl.multiple_of(start, step), size)


def packed(s):
    last = s[:, 384:512] + pltpu.roll(s[:, 896:1024], 64, 1)
    return jnp.concatenate([s[:, 0:384], s[:, 512:896], s[:, 1024:1408], last, s[:, 1408:1536]], axis=1)


def unpacked(p):
    shared = p[:, 1152:1280]
    low = lax.broadcasted_iota(jnp.int32, shared.shape, 1) < 64
    gate = jnp.where(low, shared, 0.0)
    up = jnp.where(low, pltpu.roll(shared, 64, 1), 0.0)
    return (
        jnp.concatenate([p[:, 0:384], gate], axis=1),
        jnp.concatenate([p[:, 384:768], up], axis=1),
        jnp.concatenate([p[:, 768:1152], p[:, 1280:1408]], axis=1),
    )


def kernel(
    quant, scale, cotangent, gate_q, up_q, down_q, gate_s, up_s, down_s,
    dx, gate_grad, up_grad, down_grad,
    mine_q, mine_g, mine_s, scale_rows, scales, gathered, raw, act, grad, delta, turned, w_gu, w_d, part, sib, total, z_out, z_in,
    pi_own, pi_out, r1_in, r2_own, r2_out, r2_in, r3_own, r3_out, r3_in,
    load_sem, gz, gp, gn, gf, sc, sz, sd, s1, s2, s3,
):
    hid = lax.axis_index("hid")
    mdl = lax.axis_index("mdl")
    x, z, y = hid % 4, (hid // 4) % 4, hid // 16
    core, half = mdl % 2, mdl // 2
    kinds = (z // 2, 1 - z // 2)

    def at(px, py, pz):
        return (py * 4 + pz) * 4 + px

    def near_peer(role, d):
        k = kinds[role]
        return (at((x + d * (1 - k)) % 4, (y + d * k) % 4, z), mdl)

    def line_peer(role, d):
        k = kinds[role]
        return (at((x + d * k) % 4, (y + d * (1 - k)) % 4, z), mdl)

    planes = (z, z + 1 - 2 * (z % 2), (z + 2) % 4, 3 - z)
    sibling = (hid, half * 2 + (1 - core))
    far = (hid, (1 - half) * 2 + core)

    def place(pz):
        k = pz // 2
        return k * 32 + ((y * 4 + x) * (1 - k) + (x * 4 + y) * k) * 2 + pz % 2

    def line_start(role, ahead):
        k = kinds[role]
        return k * 32 + ((y * (1 - k) + x * k) + ahead) % 4 * 8

    def line(role, ahead, first, size):
        return gathered.at[pl.ds(line_start(role, ahead) + first, size)]

    loads = [
        pltpu.make_async_copy(src, dst, load_sem.at[i])
        for i, (src, dst) in enumerate(
            [(gate_q, raw.at[0]), (up_q, raw.at[1]), (down_q, raw.at[2]), (quant, mine_q), (cotangent, mine_g)]
            + [(scale, mine_s)]
            + [(s, scale_rows.at[i]) for i, s in enumerate((gate_s, up_s, down_s))]
        )
    ]
    for i in (5, 3, 4, 6, 7, 8, 2, 0, 1):
        loads[i].start()

    barrier = pltpu.get_barrier_semaphore()
    partners = [f(0, d) for f in (near_peer, line_peer) for d in (1, 2, 3)]
    partners += [(at(x, y, p), mdl) for p in planes[1:]] + [sibling, far]
    for p in partners:
        pl.semaphore_signal(barrier, inc=1, device_id=p, device_id_type=MESH)

    pos = place(z)
    for i in range(3, 9):
        loads[i].wait()
    row = lax.broadcasted_iota(jnp.int32, (8, 1), 0)
    factor = jnp.zeros((8, 1), F32)
    for i in range(8):
        factor = jnp.where(row == i, mine_s[i], factor)
    gathered[pos] = jnp.concatenate(
        [mine_q[...].astype(F32) * factor, mine_g[...].astype(F32)], axis=0
    ).astype(BF)
    for i in range(3):
        scales[:, 8 * i:8 * i + 8] = jnp.broadcast_to(scale_rows[i], (8, H)).T

    pl.semaphore_wait(barrier, len(partners))

    sent = []

    def send(src, dst, sems, to):
        c = pltpu.make_async_remote_copy(
            src_ref=src, dst_ref=dst, send_sem=sems.at[0], recv_sem=sems.at[1],
            device_id=to, device_id_type=MESH,
        )
        c.start()
        sent.append(c)
        return c

    second = {}

    def over_near(b):
        block = gathered.at[place(planes[b])]
        second[b] = [send(block, block, gp.at[b, e - 1], near_peer(b // 2, e)) for e in (1, 3, 2)]

    own_slab = gathered.at[pos]
    over_z = {b: send(own_slab, own_slab, gz.at[b - 1], (at(x, y, planes[b]), mdl)) for b in (1, 2, 3)}
    over_near(0)

    def dequantize(i, out, row):
        loads[i].wait()

        @pl.loop(0, 7)
        def _(j):
            r = rows_at(j * 64, 64, 64)
            out[rows_at(row + j * 64, 64, 64), :] = (
                raw[i, r, :].astype(F32) * scales[r, 8 * i:8 * i + 1]
            ).astype(BF)

        out[row + H:row + HP, :] = jnp.zeros((HP - H, D), BF)

    dequantize(2, w_d, 0)
    over_z[1].wait_recv()
    over_near(1)
    dequantize(0, w_gu, 0)
    for b in (3, 2):
        over_z[b].wait_recv()
        over_near(b)
    dequantize(1, w_gu, HP)

    def own_line(role, step):
        out = []
        for i, d in enumerate((1, 3)):
            block = line(role, 0, 4 * (step ^ i), 4)
            out.append(send(block, block, gn.at[step, role, i], line_peer(role, d)))
        return out

    def pass_on(role, arrived):
        for c in arrived:
            c.wait_recv()
        out = []
        for i, d in enumerate((1, 3)):
            block = line(role, 4 - d, 4 * i, 4)
            out.append(send(block, block, gf.at[role, i], line_peer(role, d)))
        return out

    def repack(p):
        start, size = PIECES[p]
        jobs = [(p, 0, 0, 8)] if p < 2 else [(o,) + g for o in range(2) for g in GROUPS[p]]
        for role, ahead, first, n in jobs:
            base = line_start(role, ahead) + first

            @pl.loop(0, n // 2)
            def _(j):
                a = gathered[base + 2 * j].astype(F32)
                b = gathered[base + 2 * j + 1].astype(F32)
                r = rows_at(start + j * 16, 16, 16)
                act[r, :] = jnp.concatenate([a[:8], b[:8]], axis=0).astype(BF)
                grad[r, :] = jnp.concatenate([a[8:], b[8:]], axis=0).astype(BF)

            start += n * 8

    def own_rows(p):
        start, size = PIECES[p]
        return rows_at(start + core * (size // 2), size // 2, 32)

    def sums_rows(p):
        return pl.ds(PIECES[p][0] // 2, PIECES[p][1] // 2)

    def partials(p):
        repack(p)
        start, size = PIECES[p]
        r = pl.ds(start, size)

        @pl.loop(0, 4)
        def _(j):
            c = rows_at(j * 256, 256, 256)
            part[r, c] = contract_cols(act[r, :], w_gu[c, :])

        @pl.loop(0, 2)
        def _(j):
            c = rows_at(j * 256, 256, 256)
            part[r, rows_at(2 * HP + j * 256, 256, 256)] = contract_cols(grad[r, :], w_d[c, :])

        other = rows_at(start + (1 - core) * (size // 2), size // 2, 32)
        return send(part.at[other], sib.at[sums_rows(p)], sc.at[p], sibling)

    def to_far(p, arrived):
        arrived.wait_recv()
        r = sums_rows(p)
        s = part[own_rows(p), :] + sib[r, :]
        total[r, :] = s
        z_out[r, :] = packed(s).astype(BF)
        return send(z_out.at[r], z_in.at[r], sz.at[p], far)

    def activate(p, arrived):
        arrived.wait_recv()
        r = sums_rows(p)
        gate_sum, up_sum, hidden_grad = (
            total[r, i * HP:(i + 1) * HP] + v for i, v in enumerate(unpacked(z_in[r, :].astype(F32)))
        )
        gate_sigmoid = jax.nn.sigmoid(gate_sum)
        mine = own_rows(p)
        delta[mine, 0:HP] = (
            hidden_grad * up_sum * gate_sigmoid * (1.0 + gate_sum * (1.0 - gate_sigmoid))
        ).astype(BF)
        delta[mine, HP:2 * HP] = (hidden_grad * gate_sum * gate_sigmoid).astype(BF)
        delta[mine, 2 * HP:] = (gate_sum * gate_sigmoid * up_sum).astype(BF)
        return send(delta.at[mine], delta.at[mine], sd.at[p], sibling)

    over_1 = []

    def input_part(k, arrived):
        for c in arrived:
            c.wait_recv()
        r = pl.ds(k * 128, 128)

        @pl.loop(0, 8)
        def _(j):
            c = rows_at(j * 256, 256, 256)
            value = jnp.dot(delta[r, 0:2 * HP], w_gu[:, c], preferred_element_type=F32)
            if k == 0:
                pi_own[:, c] = value
            else:
                pi_out[k - 1, :, c] = value.astype(BF)

        if k > 0:
            row = 0
            for role in range(2):
                for i, (ahead, first, size) in enumerate(GROUPS[k + 1]):
                    n = size * 8
                    over_1.append(
                        send(
                            pi_out.at[k - 1, row:row + n],
                            r1_in.at[role, {3: 0, 1: 1, 2: 2}[ahead], first * 8:first * 8 + n],
                            s1.at[k - 1, role, i],
                            line_peer(role, ahead),
                        )
                    )
                    row += n

    def turn(k):
        r = pl.ds(k * 128, 128)
        for i in range(12):
            turned[i * 128:(i + 1) * 128, r] = delta[r, i * 128:(i + 1) * 128].T

    def weight_grad(i, tokens, out):
        @pl.loop(0, 8)
        def _(j):
            c = rows_at(j * 256, 256, 256)
            out[:, c] = jnp.dot(
                turned[i * HP:i * HP + H, :], tokens[:, c], preferred_element_type=F32
            ).astype(BF)

    core_copy, far_copy, ready = {}, {}, {}
    third = {}
    for c in second[0] + second[1]:
        c.wait_recv()
    third[0, 0] = own_line(0, 0)
    core_copy[0] = partials(0)
    for c in second[2] + second[3]:
        c.wait_recv()
    third[1, 0] = own_line(1, 0)
    far_copy[0] = to_far(0, core_copy[0])
    core_copy[1] = partials(1)
    fourth = pass_on(0, third[0, 0])
    far_copy[1] = to_far(1, core_copy[1])
    fourth += pass_on(1, third[1, 0])
    core_copy[2] = partials(2)
    third[0, 1] = own_line(0, 1)
    third[1, 1] = own_line(1, 1)
    ready[0] = activate(0, far_copy[0])
    far_copy[2] = to_far(2, core_copy[2])
    for c in fourth:
        c.wait_recv()
    core_copy[3] = partials(3)
    ready[1] = activate(1, far_copy[1])
    far_copy[3] = to_far(3, core_copy[3])
    input_part(0, [ready[0], ready[1]])
    for c in third[0, 1] + third[1, 1]:
        c.wait_recv()
    core_copy[4] = partials(4)
    turn(0)
    far_copy[4] = to_far(4, core_copy[4])
    for k in (1, 2, 3):
        ready[k + 1] = activate(k + 1, far_copy[k + 1])
        input_part(k, [ready[k + 1]])
        turn(k)

    weight_grad(0, act, gate_grad)
    for c in over_1:
        c.wait_recv()
    over_2 = []
    for role in range(2):
        own = pi_own[role * 64:role * 64 + 64, :]
        for k in range(3):
            own = own + r1_in[role, k].astype(F32)
        r2_own[role] = own
        r2_out[role] = own.astype(BF)
        k = kinds[role]
        me = x * (1 - k) + y * k
        for d in (2, 1, 3):
            to = rows_at((me + d) % 4 * 16, 16, 16)
            over_2.append(send(r2_out.at[role, to], r2_in.at[role, d - 1], s2.at[role, d - 1], near_peer(role, d)))
    weight_grad(1, act, up_grad)
    for c in over_2:
        c.wait_recv()
    for role in range(2):
        k = kinds[role]
        me = x * (1 - k) + y * k
        own = r2_own[role, rows_at(me * 16, 16, 16), :]
        for d in range(3):
            own = own + r2_in[role, d].astype(F32)
        for j in range(2):
            own_j = own[j * 8:j * 8 + 8]
            r3_own[2 * k + j] = own_j
            r3_out[2 * k + j] = jnp.concatenate([own_j[:, :1024], own_j[:, 1024:]], axis=0).astype(BF)
    over_3 = []
    for b in (2, 3, 1):
        over_3.append(send(r3_out.at[planes[b]], r3_in.at[b - 1], s3.at[b - 1], (at(x, y, planes[b]), mdl)))
    weight_grad(2, grad, down_grad)
    for c in over_3:
        c.wait_recv()
    own = r3_own[z]
    for d in range(3):
        got = r3_in[d].astype(F32)
        own = own + jnp.concatenate([got[:8], got[8:]], axis=1)
    dx[...] = own

    for c in sent:
        c.wait_send()


def store(dx, gate_grad, up_grad, down_grad, dx_out, gate_out, up_out, down_out, rounded, sem):
    copies = [
        pltpu.make_async_copy(src, dst, sem.at[i])
        for i, (src, dst) in enumerate([(gate_grad, gate_out), (up_grad, up_out), (down_grad, down_out)])
    ]
    for c in copies:
        c.start()
    rounded[...] = dx[...].astype(BF)
    copies.append(pltpu.make_async_copy(rounded, dx_out, sem.at[3]))
    copies[3].start()
    for c in copies:
        c.wait()


def local(
    quant_input, input_scale, grad_output, gate_quant, gate_scale, up_quant, up_scale, down_quant, down_scale,
):
    vmem = pl.BlockSpec(memory_space=pltpu.VMEM)
    hbm = pl.BlockSpec(memory_space=pltpu.HBM)
    dma = pltpu.SemaphoreType.DMA
    weight = jax.ShapeDtypeStruct((H, D), BF)
    dx, gate_grad, up_grad, down_grad = pl.pallas_call(
        kernel,
        name="ffn_backward",
        out_shape=(jax.ShapeDtypeStruct((8, D), F32), weight, weight, weight),
        in_specs=[hbm] * 9,
        out_specs=(vmem,) * 4,
        scratch_shapes=[
            pltpu.VMEM((8, D), BF),
            pltpu.VMEM((8, D), BF),
            pltpu.SMEM((8,), F32),
            pltpu.VMEM((3, 1, H), F32),
            pltpu.VMEM((H, 24), F32),
            pltpu.VMEM((64, 16, D), BF),
            pltpu.VMEM((3, H, D), BF),
            pltpu.VMEM((TOKENS, D), BF),
            pltpu.VMEM((TOKENS, D), BF),
            pltpu.VMEM((TOKENS, 3 * HP), BF),
            pltpu.VMEM((3 * HP, TOKENS), BF),
            pltpu.VMEM((2 * HP, D), BF),
            pltpu.VMEM((HP, D), BF),
            pltpu.VMEM((TOKENS, 3 * HP), F32),
            pltpu.VMEM((TOKENS // 2, 3 * HP), F32),
            pltpu.VMEM((TOKENS // 2, 3 * HP), F32),
            pltpu.VMEM((TOKENS // 2, 11 * 128), BF),
            pltpu.VMEM((TOKENS // 2, 11 * 128), BF),
            pltpu.VMEM((128, D), F32),
            pltpu.VMEM((3, 128, D), BF),
            pltpu.VMEM((2, 3, 64, D), BF),
            pltpu.VMEM((2, 64, D), F32),
            pltpu.VMEM((2, 64, D), BF),
            pltpu.VMEM((2, 3, 16, D), BF),
            pltpu.VMEM((4, 8, D), F32),
            pltpu.VMEM((4, 16, D // 2), BF),
            pltpu.VMEM((3, 16, D // 2), BF),
            dma((9,)),
            dma((3, 2)),
            dma((4, 3, 2)),
            dma((2, 2, 2, 2)),
            dma((2, 2, 2)),
            dma((5, 2)),
            dma((5, 2)),
            dma((5, 2)),
            dma((3, 2, 2, 2)),
            dma((2, 3, 2)),
            dma((3, 2)),
        ],
        compiler_params=pltpu.CompilerParams(
            collective_id=0, has_side_effects=True, vmem_limit_bytes=40 * 2**20
        ),
        cost_estimate=pl.CostEstimate(flops=9 * 10**9, bytes_accessed=12 * 10**6, transcendentals=300000),
    )(
        *(
            pltpu.with_memory_space_constraint(a, pltpu.HBM)
            for a in (
                quant_input, input_scale, grad_output, gate_quant.T, up_quant.T, down_quant,
                gate_scale.reshape(1, H), up_scale.reshape(1, H), down_scale.reshape(1, H),
            )
        )
    )
    dx, gate_grad, up_grad, down_grad = pl.pallas_call(
        store,
        name="store",
        out_shape=(pltpu.HBM((8, D), BF),) + (pltpu.HBM((H, D), BF),) * 3,
        in_specs=[vmem] * 4,
        out_specs=(hbm,) * 4,
        scratch_shapes=[pltpu.VMEM((8, D), BF), dma((4,))],
        compiler_params=pltpu.CompilerParams(vmem_limit_bytes=2**20),
    )(*(pltpu.with_memory_space_constraint(a, pltpu.VMEM) for a in (dx, gate_grad, up_grad, down_grad)))
    return (dx, gate_grad.T, up_grad.T, down_grad)


def solution(mesh):
    in_specs = (
        P("hid", "mdl"),
        P("hid"),
        P("hid", "mdl"),
        P("mdl", "hid"),
        P("hid"),
        P("mdl", "hid"),
        P("hid"),
        P("hid", "mdl"),
        P("hid"),
    )
    out_specs = (P("hid", "mdl"), P("mdl", "hid"), P("mdl", "hid"), P("hid", "mdl"))
    return jax.shard_map(local, mesh=mesh, in_specs=in_specs, out_specs=out_specs, check_vma=False)
```

time: 1230 us -> 85.3 us (0.07); the launches traced: 1210 us -> 84.5 us
  waiting for transfers between devices: 1170 us -> 0 us
  Pallas kernels: 0 us -> 83.9 us
  matrix products: 22.6 us -> 0 us
  between operations: 13.8 us -> 0.64 us
    all_gather x2 -> x0, waiting for transfers between devices: 689 us -> none  [the longest x1 346 us: local(): lax.all_gather(activations, 'hid', axis=0, tiled=True)]
    reduce_scatter x1 -> x0, waiting for transfers between devices: 353 us -> none  [local(): lax.psum_scatter(partial_input, 'hid', scatter_dimension=0, tiled=True)]
    psum x1 -> x0, waiting for transfers between devices: 128 us -> none  [local(): lax.psum((gate_part, up_part, hidden_part), 'mdl')]
    pallas_call x0 -> x2, Pallas kernels: none -> 83.9 us  [the longest x1 81.4 us: local(): pl.pallas_call(kernel, name='ffn_backward', out_shape=(jax.ShapeDtypeStru...]
    dot_general x8 -> x0, matrix products: 22.6 us -> none  [the longest x3 9.05 us: contract_cols(): lax.dot_general(left, right, (((1,), (1,)), ((), ())), preferred_element_...]
  transfers between devices with their start and end apart: 4 -> 0, of which waited for: 4 -> 0; matrix products, arithmetic and copies ran while one was open for 1% -> 0% of each run, Pallas kernels for 0% -> 0%
where the time goes in v2:
time: 85.3 us; the launch traced here: 84.5 us
  Pallas kernels  83.9 us (98%)
    pallas_call x1, Pallas kernels, local(): pl.pallas_call(kernel, name='ffn_backward', out_shape=(jax.ShapeDtypeStru...  81.4 us
    pallas_call x1, Pallas kernels, local(): pl.pallas_call(store, name='store', out_shape=(pltpu.HBM((8, D), BF),) +...  2.48 us

profile of v2, /device:TPU:6, one launch (start us, length us, event | category | flops | bytes accessed | tf_op | source)
XLA Modules:
  0.0 84.5 jit_solution(8598798561637504852)
XLA Ops:
  0.6 81.4 %ffn_backward.1 = (f32[8,2048]{1,0:T(8,128)S(1)}, bf16[448,2048]{1,0:T(8,128)(2,1)S(1)}, bf16[448,2048]{1,0:T(8,128)(2,1)S(1)}, bf16[448,2048]{1,0:T(8,128)(2,1)S(1)}) custom-call(bf16[8,2048]{1,0:T(8,128)(2,1)} %quant.1, f32[8]{0:T(128)} %scale.1, bf16[8,2048]{1,0:T(8,128)(2,1)} %cotangent.1, bf16[448,2048]{1,0:T(8,128)(2,1)} %bitcast.7, ...), custom_call_target="tpu_custom_call" | custom-call | flops 8999999488 | bytes 12000000 | tf_op jit(solution)/shard_map/ffn_backward/pallas_call | solution.py:385
  82.0 2.5 %store.1 = (bf16[8,2048]{1,0:T(8,128)(2,1)}, bf16[448,2048]{1,0:T(8,128)(2,1)}, bf16[448,2048]{1,0:T(8,128)(2,1)}, bf16[448,2048]{1,0:T(8,128)(2,1)}) custom-call(f32[8,2048]{1,0:T(8,128)S(1)} %get-tuple-element.12.dx, bf16[448,2048]{1,0:T(8,128)(2,1)S(1)} %get-tuple-element.13.gate_grad, bf16[448,2048]{1,0:T(8,128)(2,1)S(1)} %get-tuple-element.14.up_grad, ...), custom_call_target="tpu_custom_call" | custom-call | tf_op jit(solution)/shard_map/store/pallas_call | solution.py:444

commit v3 on v2

--- a/solution.py
+++ b/solution.py
@@ -12,12 +12,15 @@
 H = 448
 HP = 512
 TOKENS = 512
-PIECES = ((0, 64), (64, 64), (128, 128), (256, 128), (384, 128))
-GROUPS = {
-    2: ((3, 0, 4), (1, 4, 4)),
-    3: ((2, 0, 8),),
-    4: ((3, 4, 4), (1, 0, 4)),
-}
+STEP = 64
+PARTS = 2
+PART = D // PARTS
+GROUPS = (
+    ((0, 0, 8),),
+    ((3, 0, 4), (1, 4, 4)),
+    ((2, 0, 8),),
+    ((3, 4, 4), (1, 0, 4)),
+)
 
 
 def contract_cols(left, right):
@@ -133,8 +136,13 @@
         block = gathered.at[place(planes[b])]
         second[b] = [send(block, block, gp.at[b, e - 1], near_peer(b // 2, e)) for e in (1, 3, 2)]
 
-    own_slab = gathered.at[pos]
-    over_z = {b: send(own_slab, own_slab, gz.at[b - 1], (at(x, y, planes[b]), mdl)) for b in (1, 2, 3)}
+    over_z = {}
+
+    def to_plane(b):
+        own_slab = gathered.at[pos]
+        over_z[b] = send(own_slab, own_slab, gz.at[b - 1], (at(x, y, planes[b]), mdl))
+
+    to_plane(1)
     over_near(0)
 
     def dequantize(i, out, row):
@@ -150,6 +158,8 @@
         out[row + H:row + HP, :] = jnp.zeros((HP - H, D), BF)
 
     dequantize(2, w_d, 0)
+    to_plane(3)
+    to_plane(2)
     over_z[1].wait_recv()
     over_near(1)
     dequantize(0, w_gu, 0)
@@ -174,11 +184,18 @@
             out.append(send(block, block, gf.at[role, i], line_peer(role, d)))
         return out
 
-    def repack(p):
-        start, size = PIECES[p]
-        jobs = [(p, 0, 0, 8)] if p < 2 else [(o,) + g for o in range(2) for g in GROUPS[p]]
-        for role, ahead, first, n in jobs:
-            base = line_start(role, ahead) + first
+    def own_rows(p):
+        return rows_at(p * STEP + core * (STEP // 2), STEP // 2, STEP // 2)
+
+    def sums_rows(p):
+        return pl.ds(p * (STEP // 2), STEP // 2)
+
+    core_copy, far_copy, ready = {}, {}, {}
+
+    def partials(p):
+        start = p * STEP
+        for ahead, first, n in GROUPS[p // 2]:
+            base = line_start(p % 2, ahead) + first
 
             @pl.loop(0, n // 2)
             def _(j):
@@ -189,42 +206,31 @@
                 grad[r, :] = jnp.concatenate([a[8:], b[8:]], axis=0).astype(BF)
 
             start += n * 8
-
-    def own_rows(p):
-        start, size = PIECES[p]
-        return rows_at(start + core * (size // 2), size // 2, 32)
-
-    def sums_rows(p):
-        return pl.ds(PIECES[p][0] // 2, PIECES[p][1] // 2)
-
-    def partials(p):
-        repack(p)
-        start, size = PIECES[p]
-        r = pl.ds(start, size)
-
-        @pl.loop(0, 4)
+        r = pl.ds(p * STEP, STEP)
+
+        @pl.loop(0, 1)
         def _(j):
-            c = rows_at(j * 256, 256, 256)
+            c = rows_at(j * 1024, 1024, 1024)
             part[r, c] = contract_cols(act[r, :], w_gu[c, :])
 
-        @pl.loop(0, 2)
+        @pl.loop(0, 1)
         def _(j):
-            c = rows_at(j * 256, 256, 256)
-            part[r, rows_at(2 * HP + j * 256, 256, 256)] = contract_cols(grad[r, :], w_d[c, :])
-
-        other = rows_at(start + (1 - core) * (size // 2), size // 2, 32)
-        return send(part.at[other], sib.at[sums_rows(p)], sc.at[p], sibling)
-
-    def to_far(p, arrived):
-        arrived.wait_recv()
+            c = rows_at(j * 512, 512, 512)
+            part[r, rows_at(2 * HP + j * 512, 512, 512)] = contract_cols(grad[r, :], w_d[c, :])
+
+        other = rows_at(p * STEP + (1 - core) * (STEP // 2), STEP // 2, STEP // 2)
+        core_copy[p] = send(part.at[other], sib.at[sums_rows(p)], sc.at[p], sibling)
+
+    def to_far(p):
+        core_copy[p].wait_recv()
         r = sums_rows(p)
         s = part[own_rows(p), :] + sib[r, :]
         total[r, :] = s
         z_out[r, :] = packed(s).astype(BF)
-        return send(z_out.at[r], z_in.at[r], sz.at[p], far)
-
-    def activate(p, arrived):
-        arrived.wait_recv()
+        far_copy[p] = send(z_out.at[r], z_in.at[r], sz.at[p], far)
+
+    def activate(p):
+        far_copy[p].wait_recv()
         r = sums_rows(p)
         gate_sum, up_sum, hidden_grad = (
             total[r, i * HP:(i + 1) * HP] + v for i, v in enumerate(unpacked(z_in[r, :].astype(F32)))
@@ -236,34 +242,37 @@
         ).astype(BF)
         delta[mine, HP:2 * HP] = (hidden_grad * gate_sum * gate_sigmoid).astype(BF)
         delta[mine, 2 * HP:] = (gate_sum * gate_sigmoid * up_sum).astype(BF)
-        return send(delta.at[mine], delta.at[mine], sd.at[p], sibling)
-
-    over_1 = []
-
-    def input_part(k, arrived):
-        for c in arrived:
-            c.wait_recv()
+        ready[p] = send(delta.at[mine], delta.at[mine], sd.at[p], sibling)
+
+    over_1 = [[] for _ in range(PARTS)]
+
+    def input_part(k):
+        ready[2 * k].wait_recv()
+        ready[2 * k + 1].wait_recv()
         r = pl.ds(k * 128, 128)
-
-        @pl.loop(0, 8)
-        def _(j):
-            c = rows_at(j * 256, 256, 256)
-            value = jnp.dot(delta[r, 0:2 * HP], w_gu[:, c], preferred_element_type=F32)
+        for q in range(PARTS):
+
+            @pl.loop(q * PART // 1024, (q + 1) * PART // 1024)
+            def _(j):
+                c = rows_at(j * 1024, 1024, 1024)
+                value = jnp.dot(delta[r, 0:2 * HP], w_gu[:, c], preferred_element_type=F32)
+                if k == 0:
+                    pi_own[:, c] = value
+                else:
+                    pi_out[k - 1, :, c] = value.astype(BF)
+
             if k == 0:
-                pi_own[:, c] = value
-            else:
-                pi_out[k - 1, :, c] = value.astype(BF)
-
-        if k > 0:
+                continue
             row = 0
+            columns = slice(q * PART, (q + 1) * PART)
             for role in range(2):
-                for i, (ahead, first, size) in enumerate(GROUPS[k + 1]):
+                for i, (ahead, first, size) in enumerate(GROUPS[k]):
                     n = size * 8
-                    over_1.append(
+                    over_1[q].append(
                         send(
-                            pi_out.at[k - 1, row:row + n],
-                            r1_in.at[role, {3: 0, 1: 1, 2: 2}[ahead], first * 8:first * 8 + n],
-                            s1.at[k - 1, role, i],
+                            pi_out.at[k - 1, row:row + n, columns],
+                            r1_in.at[role, {3: 0, 1: 1, 2: 2}[ahead], first * 8:first * 8 + n, columns],
+                            s1.at[q, k - 1, role, i],
                             line_peer(role, ahead),
                         )
                     )
@@ -275,87 +284,126 @@
             turned[i * 128:(i + 1) * 128, r] = delta[r, i * 128:(i + 1) * 128].T
 
     def weight_grad(i, tokens, out):
-        @pl.loop(0, 8)
+        @pl.loop(0, 2)
         def _(j):
-            c = rows_at(j * 256, 256, 256)
+            c = rows_at(j * 1024, 1024, 1024)
             out[:, c] = jnp.dot(
                 turned[i * HP:i * HP + H, :], tokens[:, c], preferred_element_type=F32
             ).astype(BF)
 
-    core_copy, far_copy, ready = {}, {}, {}
-    third = {}
-    for c in second[0] + second[1]:
-        c.wait_recv()
+    third, fourth = {}, {}
+
+    def arrive(copies):
+        for c in copies:
+            c.wait_recv()
+
+    arrive(second[0] + second[1])
     third[0, 0] = own_line(0, 0)
-    core_copy[0] = partials(0)
-    for c in second[2] + second[3]:
-        c.wait_recv()
+    partials(0)
+    arrive(second[2] + second[3])
     third[1, 0] = own_line(1, 0)
-    far_copy[0] = to_far(0, core_copy[0])
-    core_copy[1] = partials(1)
-    fourth = pass_on(0, third[0, 0])
-    far_copy[1] = to_far(1, core_copy[1])
-    fourth += pass_on(1, third[1, 0])
-    core_copy[2] = partials(2)
+    to_far(0)
+    partials(1)
+    fourth[0] = pass_on(0, third[0, 0])
     third[0, 1] = own_line(0, 1)
+    to_far(1)
+    partials(2)
+    fourth[1] = pass_on(1, third[1, 0])
     third[1, 1] = own_line(1, 1)
-    ready[0] = activate(0, far_copy[0])
-    far_copy[2] = to_far(2, core_copy[2])
-    for c in fourth:
-        c.wait_recv()
-    core_copy[3] = partials(3)
-    ready[1] = activate(1, far_copy[1])
-    far_copy[3] = to_far(3, core_copy[3])
-    input_part(0, [ready[0], ready[1]])
-    for c in third[0, 1] + third[1, 1]:
-        c.wait_recv()
-    core_copy[4] = partials(4)
+    to_far(2)
+    partials(3)
+    activate(0)
+    to_far(3)
+    activate(1)
+    arrive(fourth[0])
+    partials(4)
+    input_part(0)
+    to_far(4)
+    arrive(fourth[1])
+    partials(5)
     turn(0)
-    far_copy[4] = to_far(4, core_copy[4])
-    for k in (1, 2, 3):
-        ready[k + 1] = activate(k + 1, far_copy[k + 1])
-        input_part(k, [ready[k + 1]])
-        turn(k)
+    to_far(5)
+    arrive(third[0, 1])
+    partials(6)
+    activate(2)
+    to_far(6)
+    arrive(third[1, 1])
+    partials(7)
+    activate(3)
+    to_far(7)
+    input_part(1)
+    turn(1)
+    activate(4)
+    activate(5)
+    input_part(2)
+    turn(2)
+    activate(6)
+    activate(7)
+    input_part(3)
+    turn(3)
+
+    def own_place(role):
+        k = kinds[role]
+        return x * (1 - k) + y * k
+
+    over_2, over_3 = {}, {}
+
+    def to_near(q):
+        for c in over_1[q]:
+            c.wait_recv()
+        columns = slice(q * PART, (q + 1) * PART)
+        over_2[q] = []
+        for role in range(2):
+            own = pi_own[role * 64:role * 64 + 64, columns]
+            for i in range(3):
+                own = own + r1_in[role, i, :, columns].astype(F32)
+            r2_own[role, :, columns] = own
+            r2_out[role, :, columns] = own.astype(BF)
+            for d in (2, 1, 3):
+                to = rows_at((own_place(role) + d) % 4 * 16, 16, 16)
+                over_2[q].append(
+                    send(
+                        r2_out.at[role, to, columns],
+                        r2_in.at[role, d - 1, :, columns],
+                        s2.at[q, role, d - 1],
+                        near_peer(role, d),
+                    )
+                )
+
+    def to_planes(q):
+        for c in over_2[q]:
+            c.wait_recv()
+        columns = slice(q * PART, (q + 1) * PART)
+        for role in range(2):
+            own = r2_own[role, rows_at(own_place(role) * 16, 16, 16), columns]
+            for d in range(3):
+                own = own + r2_in[role, d, :, columns].astype(F32)
+            for j in range(2):
+                own_j = own[j * 8:j * 8 + 8]
+                r3_own[q, 2 * kinds[role] + j] = own_j
+                r3_out[q, 2 * kinds[role] + j] = jnp.concatenate(
+                    [own_j[:, :PART // 2], own_j[:, PART // 2:]], axis=0
+                ).astype(BF)
+        over_3[q] = [
+            send(r3_out.at[q, planes[b]], r3_in.at[q, b - 1], s3.at[q, b - 1], (at(x, y, planes[b]), mdl))
+            for b in (2, 3, 1)
+        ]
 
     weight_grad(0, act, gate_grad)
-    for c in over_1:
-        c.wait_recv()
-    over_2 = []
-    for role in range(2):
-        own = pi_own[role * 64:role * 64 + 64, :]
-        for k in range(3):
-            own = own + r1_in[role, k].astype(F32)
-        r2_own[role] = own
-        r2_out[role] = own.astype(BF)
-        k = kinds[role]
-        me = x * (1 - k) + y * k
-        for d in (2, 1, 3):
-            to = rows_at((me + d) % 4 * 16, 16, 16)
-            over_2.append(send(r2_out.at[role, to], r2_in.at[role, d - 1], s2.at[role, d - 1], near_peer(role, d)))
+    to_near(0)
+    to_near(1)
     weight_grad(1, act, up_grad)
-    for c in over_2:
-        c.wait_recv()
-    for role in range(2):
-        k = kinds[role]
-        me = x * (1 - k) + y * k
-        own = r2_own[role, rows_at(me * 16, 16, 16), :]
+    to_planes(0)
+    to_planes(1)
+    weight_grad(2, grad, down_grad)
+    for q in range(PARTS):
+        for c in over_3[q]:
+            c.wait_recv()
+        own = r3_own[q, z]
         for d in range(3):
-            own = own + r2_in[role, d].astype(F32)
-        for j in range(2):
-            own_j = own[j * 8:j * 8 + 8]
-            r3_own[2 * k + j] = own_j
-            r3_out[2 * k + j] = jnp.concatenate([own_j[:, :1024], own_j[:, 1024:]], axis=0).astype(BF)
-    over_3 = []
-    for b in (2, 3, 1):
-        over_3.append(send(r3_out.at[planes[b]], r3_in.at[b - 1], s3.at[b - 1], (at(x, y, planes[b]), mdl)))
-    weight_grad(2, grad, down_grad)
-    for c in over_3:
-        c.wait_recv()
-    own = r3_own[z]
-    for d in range(3):
-        got = r3_in[d].astype(F32)
-        own = own + jnp.concatenate([got[:8], got[8:]], axis=1)
-    dx[...] = own
+            got = r3_in[q, d].astype(F32)
+            own = own + jnp.concatenate([got[:8], got[8:]], axis=1)
+        dx[:, q * PART:(q + 1) * PART] = own
 
     for c in sent:
         c.wait_send()
@@ -413,20 +461,20 @@
             pltpu.VMEM((2, 64, D), F32),
             pltpu.VMEM((2, 64, D), BF),
             pltpu.VMEM((2, 3, 16, D), BF),
-            pltpu.VMEM((4, 8, D), F32),
-            pltpu.VMEM((4, 16, D // 2), BF),
-            pltpu.VMEM((3, 16, D // 2), BF),
+            pltpu.VMEM((PARTS, 4, 8, PART), F32),
+            pltpu.VMEM((PARTS, 4, 16, PART // 2), BF),
+            pltpu.VMEM((PARTS, 3, 16, PART // 2), BF),
             dma((9,)),
             dma((3, 2)),
             dma((4, 3, 2)),
             dma((2, 2, 2, 2)),
             dma((2, 2, 2)),
-            dma((5, 2)),
-            dma((5, 2)),
-            dma((5, 2)),
-            dma((3, 2, 2, 2)),
-            dma((2, 3, 2)),
-            dma((3, 2)),
+            dma((8, 2)),
+            dma((8, 2)),
+            dma((8, 2)),
+            dma((PARTS, 3, 2, 2, 2)),
+            dma((PARTS, 2, 3, 2)),
+            dma((PARTS, 3, 2)),
         ],
         compiler_params=pltpu.CompilerParams(
             collective_id=0, has_side_effects=True, vmem_limit_bytes=40 * 2**20

time: 85.3 us -> 80.7 us (0.946)
  Pallas kernels: 83.9 us -> 79.6 us
    pallas_call x1, Pallas kernels: 81.4 us -> 77.1 us  [local(): pl.pallas_call(kernel, name='ffn_backward', out_shape=(jax.ShapeDtypeStru...]
where the time goes in v3:
time: 80.7 us; the launch traced here: 80.4 us
  Pallas kernels  79.6 us (99%)
    pallas_call x1, Pallas kernels, local(): pl.pallas_call(kernel, name='ffn_backward', out_shape=(jax.ShapeDtypeStru...  77.1 us
    pallas_call x1, Pallas kernels, local(): pl.pallas_call(store, name='store', out_shape=(pltpu.HBM((8, D), BF),) +...  2.48 us

profile of v3, /device:TPU:6, one launch (start us, length us, event | category | flops | bytes accessed | tf_op | source)
XLA Modules:
  0.0 80.4 jit_solution(10101443285303235308)
XLA Ops:
  0.6 77.1 %ffn_backward.1 = (f32[8,2048]{1,0:T(8,128)S(1)}, bf16[448,2048]{1,0:T(8,128)(2,1)S(1)}, bf16[448,2048]{1,0:T(8,128)(2,1)S(1)}, bf16[448,2048]{1,0:T(8,128)(2,1)S(1)}) custom-call(bf16[8,2048]{1,0:T(8,128)(2,1)} %quant.1, f32[8]{0:T(128)} %scale.1, bf16[8,2048]{1,0:T(8,128)(2,1)} %cotangent.1, bf16[448,2048]{1,0:T(8,128)(2,1)} %bitcast.7, ...), custom_call_target="tpu_custom_call" | custom-call | flops 8999999488 | bytes 12000000 | tf_op jit(solution)/shard_map/ffn_backward/pallas_call | solution.py:433
  77.7 2.5 %store.1 = (bf16[8,2048]{1,0:T(8,128)(2,1)}, bf16[448,2048]{1,0:T(8,128)(2,1)}, bf16[448,2048]{1,0:T(8,128)(2,1)}, bf16[448,2048]{1,0:T(8,128)(2,1)}) custom-call(f32[8,2048]{1,0:T(8,128)S(1)} %get-tuple-element.12.dx, bf16[448,2048]{1,0:T(8,128)(2,1)S(1)} %get-tuple-element.13.gate_grad, bf16[448,2048]{1,0:T(8,128)(2,1)S(1)} %get-tuple-element.14.up_grad, ...), custom_call_target="tpu_custom_call" | custom-call | tf_op jit(solution)/shard_map/store/pallas_call | solution.py:492

commit v4 on v3

--- a/solution.py
+++ b/solution.py
@@ -327,18 +327,18 @@
     partials(6)
     activate(2)
     to_far(6)
+    activate(3)
     arrive(third[1, 1])
     partials(7)
-    activate(3)
+    input_part(1)
     to_far(7)
-    input_part(1)
-    turn(1)
     activate(4)
     activate(5)
+    turn(1)
     input_part(2)
-    turn(2)
     activate(6)
     activate(7)
+    turn(2)
     input_part(3)
     turn(3)
 

time: 80.7 us -> 80.7 us (level)
  no operation moved by 1% of the time
where the time goes in v4:
time: 80.7 us; the launch traced here: 80.4 us
  Pallas kernels  79.6 us (99%)
    pallas_call x1, Pallas kernels, local(): pl.pallas_call(kernel, name='ffn_backward', out_shape=(jax.ShapeDtypeStru...  77.1 us
    pallas_call x1, Pallas kernels, local(): pl.pallas_call(store, name='store', out_shape=(pltpu.HBM((8, D), BF),) +...  2.48 us

profile of v4, /device:TPU:6, one launch (start us, length us, event | category | flops | bytes accessed | tf_op | source)
XLA Modules:
  0.0 80.4 jit_solution(4043131700571169718)
XLA Ops:
  0.6 77.1 %ffn_backward.1 = (f32[8,2048]{1,0:T(8,128)S(1)}, bf16[448,2048]{1,0:T(8,128)(2,1)S(1)}, bf16[448,2048]{1,0:T(8,128)(2,1)S(1)}, bf16[448,2048]{1,0:T(8,128)(2,1)S(1)}) custom-call(bf16[8,2048]{1,0:T(8,128)(2,1)} %quant.1, f32[8]{0:T(128)} %scale.1, bf16[8,2048]{1,0:T(8,128)(2,1)} %cotangent.1, bf16[448,2048]{1,0:T(8,128)(2,1)} %bitcast.7, ...), custom_call_target="tpu_custom_call" | custom-call | flops 8999999488 | bytes 12000000 | tf_op jit(solution)/shard_map/ffn_backward/pallas_call | solution.py:433
  77.7 2.5 %store.1 = (bf16[8,2048]{1,0:T(8,128)(2,1)}, bf16[448,2048]{1,0:T(8,128)(2,1)}, bf16[448,2048]{1,0:T(8,128)(2,1)}, bf16[448,2048]{1,0:T(8,128)(2,1)}) custom-call(f32[8,2048]{1,0:T(8,128)S(1)} %get-tuple-element.12.dx, bf16[448,2048]{1,0:T(8,128)(2,1)S(1)} %get-tuple-element.13.gate_grad, bf16[448,2048]{1,0:T(8,128)(2,1)S(1)} %get-tuple-element.14.up_grad, ...), custom_call_target="tpu_custom_call" | custom-call | tf_op jit(solution)/shard_map/store/pallas_call | solution.py:492
